TPU v7x, 512 devices: a whole 4x8x8 slice. The times are simulated.
512 devices in a mesh: walk: 32 (over z_hi, y), chol: 16 (over z_lo, x, core).
Axes of the slice: x: 4, y: 8, z: 8 (z_hi: 4, z_lo: 2; z = z_hi * 2 + z_lo), core: 2. Of those that a mesh axis runs over, the one named last changes fastest.
Arguments:
- cholesky: bfloat16 [32, 1024, 1024], P('chol'), may hold values from -0.1875 to 0.1875
- half_rotated: bfloat16 [32, 100, 1024], P('chol'), may hold values from -0.09375 to 0.09375
- green_half: bfloat16 [256, 100, 1024], P('walk', None, 'chol'), may hold values from -6 to 6
- walker: bfloat16 [256, 100, 1024], P('walk', None, 'chol'), may hold values from -6 to 6
- aux_noise: float32 [256, 32], P('walk', 'chol'), may hold values from -6 to 6
- mf_shift: float32 [4000], replicated, may hold values from -30 to 30
- chol_index: int32 [32], P('chol'), may hold values from 0 to 3999, as said below
- walker_source: int32 [256], P('walk'), may hold values from 0 to 255, each once
Outputs:
- moved_walker: bfloat16 [256, 100, 1024], P('walk', None, 'chol')
Inputs may be any that keep to these rules, and one draw needn't show every extreme that they name: `chol_index`: the 32 entries are distinct; both 0 and 3999 occur. `walker_source`: each walker is named by exactly one slot.
All inputs are finite; a program needn't handle non-finite values.
Results may differ from a plain program's by a relative error of at most 0.02.
Values may be sent and summed in bfloat16 or wider, within the bound.
A program may use at most 64 MiB of HBM per device.

v0:
```python
import jax
import jax.numpy as jnp
from jax import lax
from jax.sharding import PartitionSpec as P

field_scale = 0.1


def per_device(
    cholesky, half_rotated, green_half, walker, aux_noise, mf_shift, chol_index, walker_source
):
    groups = walker.shape[0]
    occupied = walker.shape[1]
    orbitals = cholesky.shape[1]
    vectors_here = cholesky.shape[0]
    lookup = chol_index[:, None] == lax.broadcasted_iota(
        jnp.int32, (vectors_here, mf_shift.shape[0]), 1
    )
    shift_mean = jnp.sum(jnp.where(lookup, mf_shift[None, :], 0.0), axis=1)
    green_all, walker_all = (
        lax.all_gather(green_half, "chol", axis=2, tiled=True),
        lax.all_gather(walker, "chol", axis=2, tiled=True),
    )
    bias_sum = jnp.einsum(
        "wik,gik->wg", green_all, half_rotated, preferred_element_type=jnp.float32
    )
    aux_field = aux_noise + field_scale * (bias_sum - shift_mean[None, :])

    def propagate(whole_set):
        flat_rows = whole_set.reshape(groups * occupied, orbitals)
        summed = jnp.zeros((groups, occupied, orbitals), jnp.float32)
        for vector in range(vectors_here):
            product = lax.dot_general(
                flat_rows,
                cholesky[vector],
                (((1,), (1,)), ((), ())),
                preferred_element_type=jnp.float32,
            )
            summed = summed + aux_field[:, vector][:, None, None] * product.reshape(
                groups, occupied, orbitals
            )
        return summed

    first_sum = lax.psum_scatter(
        propagate(walker_all).astype(jnp.bfloat16), "chol", scatter_dimension=2, tiled=True
    ).astype(jnp.float32)
    first_term = field_scale * first_sum
    round_all = lax.all_gather(first_term.astype(jnp.bfloat16), "chol", axis=2, tiled=True)
    second_sum = lax.psum_scatter(
        propagate(round_all).astype(jnp.bfloat16), "chol", scatter_dimension=2, tiled=True
    ).astype(jnp.float32)
    propagated = (walker.astype(jnp.float32) + first_term + 0.5 * field_scale * second_sum).astype(
        jnp.bfloat16
    )
    everyone = lax.all_gather(propagated, "walk", axis=0, tiled=True)
    return jnp.take(everyone, walker_source, axis=0)


def solution(mesh):
    placed = (
        P("chol", None, None),
        P("chol", None, None),
        P("walk", None, "chol"),
        P("walk", None, "chol"),
        P("walk", "chol"),
        P(),
        P("chol"),
        P("walk"),
    )
    return jax.shard_map(
        per_device, mesh=mesh, in_specs=placed, out_specs=P("walk", None, "chol"), check_vma=False
    )
```

profile of v0, /device:TPU:1, one launch (start us, length us, event | category | flops | bytes accessed | tf_op | source)
XLA Modules:
  0.0 404.4 jit_solution(5966741229716185733)
XLA Ops:
  6.5 0.0 copy-start
  6.5 0.0 copy-start.7
  6.5 0.0 all-gather.5.cloned.1.call-start
  6.5 1.7 copy.12
  8.2 0.0 all-gather.5.cloned.1.call-update
  8.3 0.0 all-gather.7.cloned.1.call-start
  8.3 0.7 all-gather.7.cloned.1.call-update
  9.0 0.0 reduce-scatter.3.cloned.1.call-start
  9.1 0.9 fusion.14
  10.0 44.9 %all-gather.5.cloned.1.call-done = bf16[8,100,1024]{1,0,2:T(8,128)(2,1)} async-done(((bf16[8,100,64]{1,0,2:T(8,128)(2,1)}), bf16[8,100,1024]{1,0,2:T(8,128)(2,1)}) %all-gather.5.cloned.1.call-update) | async-done | bytes 1638416 | tf_op jit(solution)/shard_map/all_gather | solution.py:21
  54.9 3.7 copy.13
  58.6 0.0 copy-done
  58.6 0.0 copy-done.7
  58.6 1.3 fusion.12
  59.9 36.3 %all-gather.7.cloned.1.call-done = bf16[8,100,1024]{1,2,0:T(8,128)(2,1)} async-done(((bf16[8,100,64]{1,2,0:T(8,128)(2,1)}), bf16[8,100,1024]{1,2,0:T(8,128)(2,1)}) %all-gather.7.cloned.1.call-update) | async-done | bytes 1638416 | tf_op jit(solution)/shard_map/all_gather | solution.py:22
  96.2 0.0 copy-start.3
  96.2 0.0 copy-start.5
  96.2 4.8 %fusion.4 = f32[8,100,1024]{1,2,0:T(8,128)S(1)} fusion(bf16[8,100,1024]{1,2,0:T(8,128)(2,1)} %all-gather.7.cloned.1.call-done, bf16[2,1024,1024]{2,1,0:T(8,128)(2,1)} %param.8), kind=kOutput, calls=%fused_computation.7 | convolution fusion | flops 1677721600 | bytes 7471104 | tf_op jit(solution)/shard_map/dot_general | solution.py:33
  101.0 0.0 copy-done.3
  101.1 0.0 copy-done.5
  101.1 4.2 %add_convert_fusion.1 = bf16[8,100,1024]{1,2,0:T(8,128)(2,1)} fusion(f32[8,100,1024]{1,2,0:T(8,128)S(1)} %fusion.4, bf16[8,100,1024]{1,2,0:T(8,128)(2,1)S(1)} %copy-done.5, f32[8]{0:T(128)S(1)} %get-tuple-element.6, f32[8]{0:T(128)S(1)} %get-tuple-element.5, bf16[2,1024,1024]{2,1,0:T(8,128)(2,1)S(1)} %copy-done.3), kind=kOutput, calls=%fused_computation.2 | convolution fusion | flops 1680998400 | bytes 10028032 | tf_op jit(solution)/shard_map/dot_general | solution.py:33
  105.2 0.0 reduce-scatter.3.cloned.1.call-update
  105.2 0.0 all-gather.9.cloned.1.call-start
  105.3 65.6 %reduce-scatter.3.cloned.1.call-done = bf16[8,100,64]{1,2,0:T(8,128)(2,1)} async-done(((bf16[8,100,1024]{1,2,0:T(8,128)(2,1)}), bf16[8,100,64]{1,2,0:T(8,128)(2,1)}) %reduce-scatter.3.cloned.1.call-update) | async-done | bytes 102416 | tf_op jit(solution)/shard_map/reduce_scatter | solution.py:44
  170.9 1.6 fusion.13
  172.5 0.0 all-gather.9.cloned.1.call-update
  172.5 0.2 reduce-scatter.5.cloned.1.call-start
  172.7 40.7 %all-gather.9.cloned.1.call-done = bf16[8,100,1024]{1,2,0:T(8,128)(2,1)} async-done(((bf16[8,100,64]{1,2,0:T(8,128)(2,1)}), bf16[8,100,1024]{1,2,0:T(8,128)(2,1)}) %all-gather.9.cloned.1.call-update) | async-done | bytes 1638416 | tf_op jit(solution)/shard_map/all_gather | solution.py:48
  213.4 0.0 copy-start.4
  213.4 0.0 copy-start.6
  213.4 4.8 %fusion.2 = f32[8,100,1024]{1,2,0:T(8,128)S(1)} fusion(bf16[8,100,1024]{1,2,0:T(8,128)(2,1)} %all-gather.9.cloned.1.call-done, bf16[2,1024,1024]{2,1,0:T(8,128)(2,1)} %param.8), kind=kOutput, calls=%fused_computation.5 | convolution fusion | flops 1677721600 | bytes 7471104 | tf_op jit(solution)/shard_map/dot_general | solution.py:33
  218.2 0.0 copy-done.4
  218.3 0.0 copy-done.6
  218.3 4.2 %add_convert_fusion = bf16[8,100,1024]{1,2,0:T(8,128)(2,1)} fusion(f32[8,100,1024]{1,2,0:T(8,128)S(1)} %fusion.2, bf16[8,100,1024]{1,2,0:T(8,128)(2,1)S(1)} %copy-done.6, f32[8]{0:T(128)S(1)} %get-tuple-element.6, f32[8]{0:T(128)S(1)} %get-tuple-element.5, bf16[2,1024,1024]{2,1,0:T(8,128)(2,1)S(1)} %copy-done.4), kind=kOutput, calls=%fused_computation.1 | convolution fusion | flops 1680998400 | bytes 10028032 | tf_op jit(solution)/shard_map/dot_general | solution.py:33
  222.4 0.0 copy-start.1
  222.4 0.0 copy-start.2
  222.4 0.0 copy-start.8
  222.4 0.0 reduce-scatter.5.cloned.1.call-update
  222.5 0.0 all-gather.11.cloned.1.call-start
  222.5 65.6 %reduce-scatter.5.cloned.1.call-done = bf16[8,100,64]{1,2,0:T(8,128)(2,1)} async-done(((bf16[8,100,1024]{1,2,0:T(8,128)(2,1)}), bf16[8,100,64]{1,2,0:T(8,128)(2,1)}) %reduce-scatter.5.cloned.1.call-update) | async-done | bytes 102416 | tf_op jit(solution)/shard_map/reduce_scatter | solution.py:49
  288.1 0.0 copy-done.1
  288.1 0.0 copy-done.2
  288.1 1.6 add_convert_fusion.2
  289.7 0.0 all-gather.11.cloned.1.call-update
  289.7 0.0 copy-done.8
  289.8 104.2 %all-gather.11.cloned.1.call-done = bf16[256,100,64]{1,2,0:T(8,128)(2,1)} async-done(((bf16[8,100,64]{1,2,0:T(8,128)(2,1)}), bf16[256,100,64]{1,2,0:T(8,128)(2,1)}) %all-gather.11.cloned.1.call-update) | async-done | bytes 3276816 | tf_op jit(solution)/shard_map/all_gather | solution.py:55
  394.0 2.8 gather_fusion
  396.8 0.7 broadcast_select_fusion
  (4 shorter events, 0.0 us)
Async XLA Ops:
  6.5 52.1 %copy-start = (bf16[2,100,1024]{2,0,1:T(2,128)(2,1)S(1)}, bf16[2,100,1024]{2,0,1:T(2,128)(2,1)}, u32[]{:S(2)}) copy-start(bf16[2,100,1024]{2,0,1:T(2,128)(2,1)} %param.9) | copy-start | bytes 1228804
  6.5 52.1 %copy-start.7 = (f32[8,2]{0,1:T(2,128)S(1)}, f32[8,2]{0,1:T(2,128)}, u32[]{:S(2)}) copy-start(f32[8,2]{0,1:T(2,128)} %param.12) | copy-start | bytes 196
  6.5 48.4 %all-gather.5.cloned.1.call-start = ((), (), s32[]{:S(2)}) async-start(), calls=%async_computation.2 | async-start | bytes 2228224 | tf_op jit(solution)/shard_map/all_gather | solution.py:21
  8.3 88.0 %all-gather.7.cloned.1.call-start = ((), (), s32[]{:S(2)}) async-start(), calls=%async_computation.3 | async-start | bytes 2228224 | tf_op jit(solution)/shard_map/all_gather | solution.py:22
  9.0 161.9 %reduce-scatter.3.cloned.1.call-start = ((), (), s32[]{:S(2)}) async-start(), calls=%async_computation.4 | async-start | bytes 2228224 | tf_op jit(solution)/shard_map/reduce_scatter | solution.py:44
  96.2 4.8 %copy-start.3 = (bf16[2,1024,1024]{2,1,0:T(8,128)(2,1)S(1)}, bf16[2,1024,1024]{2,1,0:T(8,128)(2,1)}, u32[]{:S(2)}) copy-start(bf16[2,1024,1024]{2,1,0:T(8,128)(2,1)} %param.8) | copy-start | bytes 12582916
  96.2 4.8 %copy-start.5 = (bf16[8,100,1024]{1,2,0:T(8,128)(2,1)S(1)}, bf16[8,100,1024]{1,2,0:T(8,128)(2,1)}, u32[]{:S(2)}) copy-start(bf16[8,100,1024]{1,2,0:T(8,128)(2,1)} %all-gather.7.cloned.1.call-done) | copy-start | bytes 4915204
  105.2 108.2 %all-gather.9.cloned.1.call-start = ((), (), s32[]{:S(2)}) async-start(), calls=%async_computation.5 | async-start | bytes 2228224 | tf_op jit(solution)/shard_map/all_gather | solution.py:48
  172.5 115.6 %reduce-scatter.5.cloned.1.call-start = ((), (), s32[]{:S(2)}) async-start(), calls=%async_computation.6 | async-start | bytes 2228224 | tf_op jit(solution)/shard_map/reduce_scatter | solution.py:49
  213.4 4.8 %copy-start.4 = (bf16[2,1024,1024]{2,1,0:T(8,128)(2,1)S(1)}, bf16[2,1024,1024]{2,1,0:T(8,128)(2,1)}, u32[]{:S(2)}) copy-start(bf16[2,1024,1024]{2,1,0:T(8,128)(2,1)} %param.8) | copy-start | bytes 12582916
  213.4 4.8 %copy-start.6 = (bf16[8,100,1024]{1,2,0:T(8,128)(2,1)S(1)}, bf16[8,100,1024]{1,2,0:T(8,128)(2,1)}, u32[]{:S(2)}) copy-start(bf16[8,100,1024]{1,2,0:T(8,128)(2,1)} %all-gather.9.cloned.1.call-done) | copy-start | bytes 4915204
  222.4 65.7 %copy-start.1 = (bf16[8,100,64]{1,2,0:T(8,128)(2,1)S(1)}, bf16[8,100,64]{1,2,0:T(8,128)(2,1)}, u32[]{:S(2)}) copy-start(bf16[8,100,64]{1,2,0:T(8,128)(2,1)} %param.11) | copy-start | bytes 307204
  222.4 65.7 %copy-start.2 = (bf16[8,100,64]{1,2,0:T(8,128)(2,1)S(1)}, bf16[8,100,64]{1,2,0:T(8,128)(2,1)}, u32[]{:S(2)}) copy-start(bf16[8,100,64]{1,2,0:T(8,128)(2,1)} %reduce-scatter.3.cloned.1.call-done) | copy-start | bytes 307204
  222.4 67.3 %copy-start.8 = (s32[8]{0:T(128)S(1)}, s32[8]{0:T(128)}, u32[]{:S(2)}) copy-start(s32[8]{0:T(128)} %param.15) | copy-start | bytes 100
  222.5 171.6 %all-gather.11.cloned.1.call-start = ((), (), s32[]{:S(2)}) async-start(), calls=%async_computation.7 | async-start | bytes 4325376 | tf_op jit(solution)/shard_map/all_gather | solution.py:55
Sparse Core Ops, SparseCore 0:
  9.5 45.3 all-gather.4
  57.0 39.1 all-gather.6
  105.4 65.4 reduce-scatter.2
  172.8 40.5 all-gather.8
  222.6 65.4 reduce-scatter.4
  291.1 102.8 all-gather.10
where the time goes:
time: 405 us; the launch traced here: 404 us
  waiting for transfers between devices  358 us (88%)
  matrix products  19.2 us (5%)
  between operations  13.6 us (3%)
  local copies, waits for them, and re-layouts  8.18 us (2%)
  other arithmetic  4.92 us (1%)
    all_gather x1, waiting for transfers between devices, per_device(): everyone = lax.all_gather(propagated, 'walk', axis=0, tiled=True)  104 us
    reduce_scatter x1, waiting for transfers between devices, per_device(): lax.psum_scatter(propagate(walker_all).astype(jnp.bfloat16), 'chol', scat...  65.6 us
    reduce_scatter x1, waiting for transfers between devices, per_device(): lax.psum_scatter(propagate(round_all).astype(jnp.bfloat16), 'chol', scatt...  65.6 us
    all_gather x1, waiting for transfers between devices, per_device(): lax.all_gather(green_half, 'chol', axis=2, tiled=True)  44.9 us
    all_gather x1, waiting for transfers between devices, per_device(): lax.all_gather(first_term.astype(jnp.bfloat16), 'chol', axis=2, tiled=True)  40.7 us
    all_gather x1, waiting for transfers between devices, per_device(): lax.all_gather(walker, 'chol', axis=2, tiled=True)  36.3 us
    dot_general x4, matrix products, propagate(): lax.dot_general(flat_rows, cholesky[vector], (((1,), (1,)), ((), ())), pr...  17.9 us
  transfers between devices with their start and end apart: 6, of which 6 were waited for; matrix products, arithmetic and copies ran while one was open for 1% of the time, Pallas kernels for 0%

commit v1 on v0

v1 whole, which is shorter than its diff:
```python
import jax
import jax.numpy as jnp
from jax import lax
from jax.experimental import pallas as pl
from jax.experimental.pallas import tpu as pltpu
from jax.sharding import PartitionSpec as P

MESH = pl.DeviceIdType.MESH
field_scale = 0.1
CHUNKS = 4
TILES = 8
WALK = 32


def body(
    chol_ref, half_ref, green_ref, walker_ref, noise_ref, mean_ref, index_ref, source_ref,
    out_ref,
    lst, xg1, xg2, part, hop1, hop2, hopz_src, hopz, first, acc, hrg, gp, fb, btile, final,
    zsend, zrecv, ysend, yrecv, stile, sall,
    ag_s, ag_r, rs_s, rs_r, hr_s, hr_r, b_s, b_r, w_s, w_r, z_s, z_r, y_s, y_r, misc,
):
    walk = lax.axis_index("walk")
    chol = lax.axis_index("chol")
    core = chol % 2
    chip = chol // 2
    x, z = chip % 4, chip // 4
    xn, xp, xf, zo = (x + 1) % 4, (x + 3) % 4, (x + 2) % 4, 1 - z

    def at(zz, xx, cc):
        return zz * 8 + xx * 2 + cc

    dev_z = {"chol": at(zo, x, core)}
    dev_n = {"chol": at(z, xn, core)}
    dev_p = {"chol": at(z, xp, core)}
    dev_sib = {"chol": at(z, x, 1 - core)}

    own_l = pltpu.make_async_copy(
        chol_ref.at[:, :, core], lst.at[pl.ds(2 * core, 2)], misc.at[0]
    )
    own_l.start()
    own_h = pltpu.make_async_copy(
        half_ref.at[:, :, pl.ds(pl.multiple_of(chip * 128, 128), 128)],
        hrg.at[chip, :, pl.ds(0, 112)],
        misc.at[1],
    )
    own_h.start()

    barrier = pltpu.get_barrier_semaphore()

    @pl.loop(1, 16)
    def _(d):
        pl.semaphore_signal(
            barrier, inc=1, device_id={"chol": (chol + d) % 16}, device_id_type=MESH
        )

    @pl.loop(1, WALK)
    def _(d):
        pl.semaphore_signal(
            barrier, inc=1, device_id={"walk": (walk + d) % WALK}, device_id_type=MESH
        )

    gp[:, core] = jnp.zeros((8, 64, 128), jnp.bfloat16)
    gp[:, core, :, 0:100] = green_ref[...]
    xg1[:, chol] = jnp.zeros((TILES, 64, 128), jnp.bfloat16)
    xg1[:, chol, :, 0:100] = walker_ref[...]
    hrg[:, :, 112:128, :] = jnp.zeros((8, 2, 16, 128), jnp.bfloat16)

    row8 = lax.broadcasted_iota(jnp.int32, (8, 128), 0)
    lane8 = lax.broadcasted_iota(jnp.int32, (8, 128), 1)
    ids = jnp.zeros((8, 128), jnp.int32)
    for s in range(8):
        value = source_ref[s]
        ids = jnp.where(row8 == s, (value // 8) * 16 + value % 8, ids)
    stile[...] = ids
    sall[walk] = ids

    pl.semaphore_wait(barrier, 15 + WALK - 1)

    def remote(src, dst, ssem, rsem, dev):
        return pltpu.make_async_remote_copy(
            src_ref=src, dst_ref=dst, send_sem=ssem, recv_sem=rsem,
            device_id=dev, device_id_type=MESH,
        )

    g_copy = remote(gp.at[:, core], gp.at[:, core], misc.at[2], misc.at[3], dev_sib)
    g_copy.start()
    g_got = remote(gp.at[:, 1 - core], gp.at[:, 1 - core], misc.at[2], misc.at[3], dev_sib)

    others = ((0, 1), (0, 3), (1, 0), (1, 1), (1, 3), (0, 2), (1, 2))

    def hr_copy(k, dz, dx):
        there = ((z + dz) % 2) * 4 + (x + dx) % 4
        return remote(
            half_ref.at[:, :, pl.ds(pl.multiple_of(there * 128, 128), 128)],
            hrg.at[chip, :, pl.ds(0, 112)],
            hr_s.at[k], hr_r.at[k], {"chol": there * 2 + core},
        )

    def hr_got(k, dz, dx):
        there = ((z + dz) % 2) * 4 + (x + 4 - dx) % 4
        return remote(
            hrg.at[there, :, pl.ds(0, 112)], hrg.at[there, :, pl.ds(0, 112)],
            hr_s.at[k], hr_r.at[k], dev_z,
        )

    for k, (dz, dx) in enumerate(others):
        hr_copy(k, dz, dx).start()

    l_copy = remote(
        chol_ref.at[:, :, 1 - core], lst.at[pl.ds(2 * core, 2)], misc.at[4], misc.at[5], dev_sib
    )
    l_got = remote(
        lst.at[pl.ds(2 * (1 - core), 2)], lst.at[pl.ds(2 * (1 - core), 2)],
        misc.at[4], misc.at[5], dev_sib,
    )

    def ag_parts(xg, j, kind, sending, cc):
        full, low, high = pl.ds(2 * j, 2), 2 * j, 2 * j + 1
        send = {
            0: (full, z, x), 1: (full, z, x), 2: (full, z, x),
            3: (full, zo, x), 4: (full, zo, x),
            5: (low, z, xp), 6: (high, z, xn), 7: (low, zo, xp), 8: (high, zo, xn),
        }
        recv = {
            0: (full, zo, x), 1: (full, z, xp), 2: (full, z, xn),
            3: (full, zo, xp), 4: (full, zo, xn),
            5: (low, z, xf), 6: (high, z, xf), 7: (low, zo, xf), 8: (high, zo, xf),
        }
        tiles, zz, xx = (send if sending else recv)[kind]
        return xg.at[tiles, at(zz, xx, cc)]

    def ag_dev(kind):
        return dev_z if kind == 0 else (dev_n if kind in (1, 3, 5, 7) else dev_p)

    def ag_send(ph, xg, j, kind):
        ref = ag_parts(xg, j, kind, True, core)
        return remote(ref, ref, ag_s.at[ph, j, kind], ag_r.at[ph, j, kind], ag_dev(kind))

    def ag_got(ph, xg, j, kind):
        ref = ag_parts(xg, j, kind, False, core)
        return remote(ref, ref, ag_s.at[ph, j, kind], ag_r.at[ph, j, kind], ag_dev(kind))

    def sib_part(xg, j, kind, cc):
        if kind == 9:
            return xg.at[pl.ds(2 * j, 2), at(z, x, cc)]
        return ag_parts(xg, j, kind - 10, False, cc)

    def sib(ph, xg, j, kind, cc):
        ref = sib_part(xg, j, kind, cc)
        return remote(ref, ref, ag_s.at[ph, j, kind], ag_r.at[ph, j, kind], dev_sib)

    def ag_start(ph, xg, j):
        for kind in (1, 2, 0):
            ag_send(ph, xg, j, kind).start()
        sib(ph, xg, j, 9, core).start()

    def ag_arrive(ph, xg, j, kind, onward):
        ag_got(ph, xg, j, kind).wait_recv()
        for k in onward:
            ag_send(ph, xg, j, k).start()
        sib(ph, xg, j, 10 + kind, core).start()

    def ag_fwd1(ph, xg, j):
        ag_arrive(ph, xg, j, 0, (3, 4))
        ag_arrive(ph, xg, j, 1, (5,))
        ag_arrive(ph, xg, j, 2, (6,))

    def ag_fwd2(ph, xg, j):
        ag_arrive(ph, xg, j, 3, (7,))
        ag_arrive(ph, xg, j, 4, (8,))

    def ag_fwd3(ph, xg, j):
        for kind in (5, 6, 7, 8):
            ag_arrive(ph, xg, j, kind, ())

    def ag_fin(ph, xg, j):
        for kind in range(9, 19):
            sib(ph, xg, j, kind, 1 - core).wait_recv()

    def rs_copy(ph, j, kind):
        if kind == 0:
            src, dst, dev = part.at[ph, j, :, xf, 0], hop1.at[ph, j, 0], dev_n
        elif kind == 1:
            src, dst, dev = part.at[ph, j, :, xf, 1], hop1.at[ph, j, 1], dev_p
        elif kind == 2:
            src, dst, dev = part.at[ph, j, :, xn], hop2.at[ph, j, 0], dev_n
        elif kind == 3:
            src, dst, dev = part.at[ph, j, :, xp], hop2.at[ph, j, 1], dev_p
        else:
            src, dst, dev = hopz_src.at[ph, j], hopz.at[ph, j], dev_z
        return remote(src, dst, rs_s.at[ph, j, kind], rs_r.at[ph, j, kind], dev)

    f32 = jnp.float32

    def rs_start(ph, j):
        rs_copy(ph, j, 0).start()
        rs_copy(ph, j, 1).start()

    def rs_mid(ph, j):
        for kind, where in ((0, xn), (1, xp)):
            rs_copy(ph, j, kind).wait_recv()
            part[ph, j, :, where, kind] = (
                part[ph, j, :, where, kind].astype(f32) + hop1[ph, j, kind].astype(f32)
            ).astype(jnp.bfloat16)
            rs_copy(ph, j, kind + 2).start()

    def summed(ph, j, zz):
        return (
            part[ph, j, zz, x].astype(f32)
            + hop2[ph, j, 0, zz].astype(f32)
            + hop2[ph, j, 1, zz].astype(f32)
        )

    def rs_last(ph, j):
        rs_copy(ph, j, 2).wait_recv()
        rs_copy(ph, j, 3).wait_recv()
        hopz_src[ph, j] = summed(ph, j, zo).astype(jnp.bfloat16)
        rs_copy(ph, j, 4).start()

    def rs_fin(ph, j):
        rs_copy(ph, j, 4).wait_recv()
        return summed(ph, j, z) + hopz[ph, j].astype(f32)

    def matmul(ph, xg, j):
        both = jnp.concatenate(
            [xg[2 * j].reshape(1024, 128), xg[2 * j + 1].reshape(1024, 128)], axis=1
        )
        for g in range(4):
            rows = lst[g].reshape(512, 1024)
            product = jnp.dot(rows, both, preferred_element_type=f32)
            scale = jnp.concatenate(
                [fb[g, pl.ds(2 * j, 1), :], fb[g, pl.ds(2 * j + 1, 1), :]], axis=1
            )
            if g == 0:
                acc[...] = product * scale
            else:
                acc[...] += product * scale
        for zz in range(2):
            for xx in range(4):
                for t in range(2):
                    part[ph, j, zz, xx, t] = acc[
                        pl.ds((zz * 4 + xx) * 64, 64), pl.ds(128 * t, 128)
                    ].astype(jnp.bfloat16)

    for j in range(CHUNKS):
        ag_start(0, xg1, j)
    l_copy.start()

    def s_copy(d, sending):
        there = (walk + d) % WALK if sending else (walk + WALK - d) % WALK
        return remote(
            stile, sall.at[walk] if sending else sall.at[there],
            w_s.at[d], w_r.at[d], {"walk": there},
        )

    @pl.loop(1, WALK)
    def _(d):
        s_copy(d, True).start()

    own_h.wait()
    g_got.wait_recv()
    for k, (dz, dx) in enumerate(others):
        hr_got(k, dz, dx).wait_recv()

    eye = (
        lax.broadcasted_iota(jnp.int32, (128, 128), 0)
        == lax.broadcasted_iota(jnp.int32, (128, 128), 1)
    ).astype(f32)
    greens = gp[...].reshape(1024, 128)

    def one_vector(v, tile):
        source, which = v // 2, v % 2
        product = jnp.dot(greens, hrg[source, which], preferred_element_type=f32)
        picked = jnp.sum(product.reshape(8, 128, 128) * eye[None], axis=1)
        value = jnp.sum(picked, axis=1, keepdims=True)
        return jnp.where(lane8 == source * 4 + core * 2 + which, field_scale * value, tile)

    tile = lax.fori_loop(0, 16, one_vector, jnp.zeros((8, 128), f32))
    for which in range(2):
        shift = mean_ref[index_ref[which]]
        for w in range(8):
            tile = tile + jnp.where(
                (row8 == w) & (lane8 == chol * 2 + which),
                noise_ref[which, w] - field_scale * shift, 0.0,
            )
    btile[chol] = tile

    def b_copy(d, sending):
        there = (chol + d) % 16 if sending else (chol + 16 - d) % 16
        slot = chol if sending else there
        return remote(
            btile.at[slot], btile.at[slot], b_s.at[d], b_r.at[d], {"chol": there}
        )

    @pl.loop(1, 16)
    def _(d):
        b_copy(d, True).start()

    for j in range(CHUNKS):
        ag_fwd1(0, xg1, j)
        if j >= 1:
            ag_fwd2(0, xg1, j - 1)
        if j >= 2:
            ag_fwd3(0, xg1, j - 2)
    ag_fwd2(0, xg1, CHUNKS - 1)
    ag_fwd3(0, xg1, CHUNKS - 2)

    @pl.loop(1, 16)
    def _(d):
        b_copy(d, False).wait_recv()

    field = btile[0]
    for c in range(1, 16):
        field = field + btile[c]
    for g in range(4):
        value = jnp.sum(
            jnp.where(lane8 == chip * 4 + g, field, 0.0), axis=1, keepdims=True
        )
        fb[g] = jnp.broadcast_to(value, (8, 128))

    own_l.wait()
    l_got.wait_recv()

    for t in range(CHUNKS + 9):
        def chunk(lag):
            return t - lag if 0 <= t - lag < CHUNKS else None

        j = chunk(9)
        if j is not None:
            second = rs_fin(1, j)
            moved = (
                xg1[pl.ds(2 * j, 2), chol].astype(f32)
                + first[pl.ds(2 * j, 2)]
                + (0.5 * field_scale) * second
            )
            final[pl.ds(128 * j, 128)] = moved.reshape(128, 128)
        j = chunk(8)
        if j is not None:
            rs_last(1, j)
        j = chunk(7)
        if j is not None:
            rs_mid(1, j)
        j = chunk(5)
        if j is not None:
            ag_fwd2(1, xg2, j)
        j = chunk(4)
        if j is not None:
            ag_fwd1(1, xg2, j)
        j = chunk(3)
        if j is not None:
            term = field_scale * rs_fin(0, j)
            first[pl.ds(2 * j, 2)] = term
            xg2[pl.ds(2 * j, 2), chol] = term.astype(jnp.bfloat16)
            ag_start(1, xg2, j)
        j = chunk(2)
        if j is not None:
            rs_last(0, j)
        j = chunk(1)
        if j is not None:
            rs_mid(0, j)
        j = chunk(0)
        if j is not None:
            if j == CHUNKS - 1:
                ag_fwd3(0, xg1, j)
            ag_fin(0, xg1, j)
            matmul(0, xg1, j)
            rs_start(0, j)
        j = chunk(6)
        if j is not None:
            ag_fwd3(1, xg2, j)
            ag_fin(1, xg2, j)
            matmul(1, xg2, j)
            rs_start(1, j)

    for p in range(WALK):
        zsend[p] = jnp.concatenate(
            [final[pl.ds(2 * p, 8, stride=64), :], final[pl.ds(2 * p + 1, 8, stride=64), :]],
            axis=0,
        ).astype(jnp.bfloat16)
    zrecv[walk] = zsend[walk]

    def z_copy(d, sending):
        there = (walk + d) % WALK if sending else (walk + WALK - d) % WALK
        return remote(
            zsend.at[there], zrecv.at[walk] if sending else zrecv.at[there],
            z_s.at[d], z_r.at[d], {"walk": there},
        )

    def y_copy(d, sending):
        there = (walk + d) % WALK if sending else (walk + WALK - d) % WALK
        return remote(
            ysend.at[there], yrecv.at[walk] if sending else yrecv.at[there],
            y_s.at[d], y_r.at[d], {"walk": there},
        )

    @pl.loop(1, WALK)
    def _(d):
        z_copy(d, True).start()

    @pl.loop(1, WALK)
    def _(d):
        s_copy(d, False).wait_recv()

    low = sall[...]
    wanted = jnp.stack([low, low + 8], axis=1).reshape(WALK * 16, 128)
    lanes = lax.broadcasted_iota(jnp.int32, (WALK * 16, 128), 1)
    picks = [
        jnp.where(wanted == lanes + 128 * b, 1.0, 0.0).astype(jnp.bfloat16) for b in range(4)
    ]

    @pl.loop(1, WALK)
    def _(d):
        z_copy(d, False).wait_recv()

    here = zrecv[...].reshape(WALK * 16, 128)
    taken = jnp.dot(picks[0], here[0:128], preferred_element_type=f32)
    for b in range(1, 4):
        taken = taken + jnp.dot(
            picks[b], here[128 * b : 128 * (b + 1)], preferred_element_type=f32
        )
    ysend[...] = taken.astype(jnp.bfloat16).reshape(WALK, 16, 128)
    yrecv[walk] = ysend[walk]

    @pl.loop(1, WALK)
    def _(d):
        y_copy(d, True).start()

    g_copy.wait_send()
    l_copy.wait_send()
    for k, (dz, dx) in enumerate(others):
        hr_copy(k, dz, dx).wait_send()

    @pl.loop(1, 16)
    def _(d):
        b_copy(d, True).wait_send()

    for ph, xg in ((0, xg1), (1, xg2)):
        for j in range(CHUNKS):
            for kind in range(9):
                ag_send(ph, xg, j, kind).wait_send()
            for kind in range(9, 19):
                sib(ph, xg, j, kind, core).wait_send()
            for kind in range(5):
                rs_copy(ph, j, kind).wait_send()

    @pl.loop(1, WALK)
    def _(d):
        s_copy(d, True).wait_send()
        z_copy(d, True).wait_send()

    @pl.loop(1, WALK)
    def _(d):
        y_copy(d, False).wait_recv()

    for p in range(WALK):
        both = yrecv[p].astype(f32)
        final[pl.ds(2 * p, 8, stride=64), :] = both[0:8]
        final[pl.ds(2 * p + 1, 8, stride=64), :] = both[8:16]
    out_ref[...] = final[...].reshape(8, 64, 128)[:, :, 0:100].astype(jnp.bfloat16)

    @pl.loop(1, WALK)
    def _(d):
        y_copy(d, True).wait_send()


def per_device(
    cholesky, half_rotated, green_half, walker, aux_noise, mf_shift, chol_index, walker_source
):
    bf16, f32 = jnp.bfloat16, jnp.float32
    vmem = pl.BlockSpec(memory_space=pltpu.VMEM)
    smem = pl.BlockSpec(memory_space=pltpu.SMEM)
    anyw = pl.BlockSpec(memory_space=pl.ANY)
    V = pltpu.VMEM
    D = pltpu.SemaphoreType.DMA
    moved = pl.pallas_call(
        body,
        out_shape=jax.ShapeDtypeStruct((8, 64, 100), bf16),
        in_specs=[anyw, anyw, vmem, vmem, smem, smem, smem, smem],
        out_specs=vmem,
        scratch_shapes=[
            V((4, 8, 64, 1024), bf16),
            V((TILES, 16, 64, 128), bf16),
            V((TILES, 16, 64, 128), bf16),
            V((2, CHUNKS, 2, 4, 2, 64, 128), bf16),
            V((2, CHUNKS, 2, 2, 64, 128), bf16),
            V((2, CHUNKS, 2, 2, 2, 64, 128), bf16),
            V((2, CHUNKS, 2, 64, 128), bf16),
            V((2, CHUNKS, 2, 64, 128), bf16),
            V((TILES, 64, 128), f32),
            V((512, 256), f32),
            V((8, 2, 128, 128), bf16),
            V((8, 2, 64, 128), bf16),
            V((4, 8, 128), f32),
            V((16, 8, 128), f32),
            V((512, 128), f32),
            V((WALK, 16, 128), bf16),
            V((WALK, 16, 128), bf16),
            V((WALK, 16, 128), bf16),
            V((WALK, 16, 128), bf16),
            V((8, 128), jnp.int32),
            V((WALK, 8, 128), jnp.int32),
            D((2, CHUNKS, 19)),
            D((2, CHUNKS, 19)),
            D((2, CHUNKS, 5)),
            D((2, CHUNKS, 5)),
            D((7,)),
            D((7,)),
            D((16,)),
            D((16,)),
            D((WALK,)),
            D((WALK,)),
            D((WALK,)),
            D((WALK,)),
            D((WALK,)),
            D((WALK,)),
            D((6,)),
        ],
        compiler_params=pltpu.CompilerParams(
            collective_id=0, has_side_effects=True, vmem_limit_bytes=40 * 1024 * 1024
        ),
        cost_estimate=pl.CostEstimate(
            flops=8_600_000_000, bytes_accessed=6_000_000, transcendentals=0
        ),
    )(
        cholesky.reshape(2, 8, 2, 64, 1024),
        jnp.pad(half_rotated, ((0, 0), (0, 12), (0, 0))),
        jnp.transpose(green_half, (0, 2, 1)),
        jnp.transpose(walker, (0, 2, 1)),
        jnp.transpose(aux_noise, (1, 0)),
        mf_shift,
        chol_index,
        walker_source,
    )
    return jnp.transpose(moved, (0, 2, 1))


def solution(mesh):
    placed = (
        P("chol", None, None),
        P("chol", None, None),
        P("walk", None, "chol"),
        P("walk", None, "chol"),
        P("walk", "chol"),
        P(),
        P("chol"),
        P("walk"),
    )
    return jax.shard_map(
        per_device, mesh=mesh, in_specs=placed, out_specs=P("walk", None, "chol"), check_vma=False
    )
```

time: 405 us -> 131 us (0.32)
  waiting for transfers between devices: 358 us -> 0 us
  Pallas kernels: 0 us -> 121 us
  matrix products: 19.2 us -> 0 us
  between operations: 13.6 us -> 0.04 us
  other arithmetic: 4.92 us -> 0 us
    all_gather x4 -> x0, waiting for transfers between devices: 226 us -> none  [the longest x1 104 us: per_device(): everyone = lax.all_gather(propagated, 'walk', axis=0, tiled=True)]
    reduce_scatter x2 -> x0, waiting for transfers between devices: 131 us -> none  [the longest x1 65.6 us: per_device(): lax.psum_scatter(propagate(walker_all).astype(jnp.bfloat16), 'chol', scat...]
    pallas_call x0 -> x1, Pallas kernels: none -> 121 us  [per_device(): pl.pallas_call(body, out_shape=jax.ShapeDtypeStruct((8, 64, 100), bf16),...]
    dot_general x5 -> x0, matrix products: 19.2 us -> none  [the longest x4 17.9 us: propagate(): lax.dot_general(flat_rows, cholesky[vector], (((1,), (1,)), ((), ())), pr...]
    unnamed x19 -> x16, local copies, waits for them, and re-layouts: 1.73 us -> 8.43 us
  transfers between devices with their start and end apart: 6 -> 0, of which waited for: 6 -> 0; matrix products, arithmetic and copies ran while one was open for 1% -> 0% of each run, Pallas kernels for 0% -> 0%
where the time goes in v1:
time: 131 us; the launch traced here: 129 us
  Pallas kernels  121 us (92%)
  local copies, waits for them, and re-layouts  8.47 us (6%)
    pallas_call x1, Pallas kernels, per_device(): pl.pallas_call(body, out_shape=jax.ShapeDtypeStruct((8, 64, 100), bf16),...  121 us
    unnamed x16, local copies, waits for them, and re-layouts  8.43 us

profile of v1, /device:TPU:1, one launch (start us, length us, event | category | flops | bytes accessed | tf_op | source)
XLA Modules:
  0.0 129.4 jit_solution(10495710036381182892)
XLA Ops:
  0.0 1.1 copy.9
  1.1 0.0 copy-start
  1.1 2.2 %copy-done = bf16[2,1024,1024]{2,1,0:T(8,128)(2,1)S(1)} copy-done((bf16[2,1024,1024]{2,1,0:T(8,128)(2,1)S(1)}, bf16[2,1024,1024]{2,1,0:T(8,128)(2,1)}, u32[]{:S(2)}) %copy-start) | copy-done | bytes 4194328
  3.3 0.0 copy-start.1
  3.3 0.9 copy-done.1
  4.2 0.0 copy-start.2
  4.2 0.9 copy-done.2
  5.1 0.0 copy-start.3
  5.1 0.7 copy-done.3
  5.9 0.0 copy-start.4
  5.9 0.7 copy-done.4
  6.5 0.0 copy-start.5
  6.5 0.7 copy-done.5
  7.2 0.0 copy-start.6
  7.2 0.7 copy-done.6
  7.8 120.9 %shard_map.82 = bf16[8,64,100]{2,1,0:T(8,128)(2,1)S(1)} custom-call(bf16[2,8,2,64,1024]{4,3,2,1,0:T(8,128)(2,1)S(1)} %bitcast.6, bf16[2,112,1024]{2,1,0:T(8,128)(2,1)S(1)} %pad.4.half_ref, bf16[8,64,100]{2,1,0:T(8,128)(2,1)S(1)} %bitcast.7, bf16[8,64,100]{2,1,0:T(8,128)(2,1)S(1)} %bitcast.8, f32[2,8]{1,0:T(2,128)S(1)} %bitcast.9, f32[4000]{0:T(1024)S(1)} %copy-done.3, ...), custom_call_target="tpu_custom_call" | custom-call | flops 8600000512 | bytes 6000000 | tf_op jit(solution)/shard_map/pallas_call | solution.py:475
  128.7 0.7 copy.11
  (1 shorter events, 0.0 us)
Async XLA Ops:
  1.1 2.2 %copy-start = (bf16[2,1024,1024]{2,1,0:T(8,128)(2,1)S(1)}, bf16[2,1024,1024]{2,1,0:T(8,128)(2,1)}, u32[]{:S(2)}) copy-start(bf16[2,1024,1024]{2,1,0:T(8,128)(2,1)} %param.8) | copy-start | bytes 12582916
  3.3 0.9 copy-start.1
  4.2 0.9 copy-start.2
  5.1 0.7 copy-start.3
  5.9 0.7 copy-start.4
  6.5 0.7 copy-start.5
  7.2 0.7 copy-start.6

commit v2 on v0

v2 whole, which is shorter than its diff:
```python
import jax
import jax.numpy as jnp
from jax import lax
from jax.experimental import pallas as pl
from jax.experimental.pallas import tpu as pltpu
from jax.sharding import PartitionSpec as P

MESH = pl.DeviceIdType.MESH
field_scale = 0.1
TILES = 7
SPANS = ((0, 2), (2, 2), (4, 2), (6, 1))
CHUNKS = len(SPANS)
WALK = 32
OCC = 100
OTHERS = ((1, 2), (0, 2), (1, 1), (1, 3), (0, 1), (0, 3), (1, 0))


def body(
    chol_ref, half_ref, green_ref, walker_ref, noise_ref, mean_ref, index_ref, source_ref,
    out_ref,
    lst, xg1, xg2, part, got, first, acc, hrg, gp, fb, btile, done, final,
    zsend, zrecv, ysend, yrecv, stile, sall, picks,
    green_in, walker_in, noise_in, mean_in, index_in, source_in,
    ag_s, ag_r, sib_s, sib_r, rs_s, rs_r, hr_s, hr_r, b_s, b_r, w_s, w_r, z_s, z_r, y_s, y_r,
    misc, in_sem,
):
    f32, bf16 = jnp.float32, jnp.bfloat16
    walk = lax.axis_index("walk")
    chol = lax.axis_index("chol")
    core = chol % 2
    chip = chol // 2
    x, z = chip % 4, chip // 4
    dev_sib = {"chol": chip * 2 + 1 - core}

    barrier = pltpu.get_barrier_semaphore()

    @pl.loop(1, WALK)
    def _(d):
        pl.semaphore_signal(
            barrier, inc=1, device_id={"walk": (walk + d) % WALK}, device_id_type=MESH
        )

    @pl.loop(1, 16)
    def _(d):
        pl.semaphore_signal(
            barrier, inc=1, device_id={"chol": (chol + d) % 16}, device_id_type=MESH
        )

    loads = [
        pltpu.make_async_copy(a, b, in_sem.at[n])
        for n, (a, b) in enumerate(
            (
                (source_ref, source_in), (walker_ref, walker_in), (green_ref, green_in),
                (index_ref, index_in), (noise_ref, noise_in), (mean_ref, mean_in),
            )
        )
    ]
    for load in loads:
        load.start()
    own_h = pltpu.make_async_copy(
        half_ref.at[:, :, pl.ds(pl.multiple_of(chip * 128, 128), 128)],
        hrg.at[chip, :, pl.ds(0, 112)],
        misc.at[1],
    )
    own_h.start()
    own_l = pltpu.make_async_copy(
        chol_ref.at[:, :, core], lst.at[pl.ds(2 * core, 2)], misc.at[0]
    )
    own_l.start()

    hrg[:, :, 112:128, :] = jnp.zeros((8, 2, 16, 128), bf16)

    row8 = lax.broadcasted_iota(jnp.int32, (8, 128), 0)
    lane8 = lax.broadcasted_iota(jnp.int32, (8, 128), 1)
    loads[0].wait()
    ids = jnp.zeros((8, 128), jnp.int32)
    for s in range(8):
        value = source_in[s]
        ids = jnp.where(row8 == s, (value // 8) * 16 + value % 8, ids)
    stile[...] = ids
    sall[walk] = ids

    loads[1].wait()
    done[...] = jnp.zeros_like(done)
    done[:, :, 0:OCC] = walker_in[...].astype(f32)
    lanes = lax.broadcasted_iota(jnp.int32, (64, 128), 1)
    shifted = [
        pltpu.roll(done[w], (OCC * w) % 128, 1) if w else done[w] for w in range(8)
    ]
    for t in range(TILES):
        tile = jnp.zeros((64, 128), f32)
        for w in range(8):
            low, high = OCC * w - 128 * t, OCC * (w + 1) - 128 * t
            if high > 0 and low < 128:
                tile = jnp.where((lanes >= low) & (lanes < high), shifted[w], tile)
        xg1[t, chol] = tile.astype(bf16)
    loads[2].wait()
    gp[:, core] = jnp.zeros((8, 64, 128), bf16)
    gp[:, core, :, 0:OCC] = green_in[...]

    pl.semaphore_wait(barrier, 15 + WALK - 1)

    def remote(src, dst, ssem, rsem, dev):
        return pltpu.make_async_remote_copy(
            src_ref=src, dst_ref=dst, send_sem=ssem, recv_sem=rsem,
            device_id=dev, device_id_type=MESH,
        )

    def chip_to(dz, dx):
        return ((z + dz) % 2) * 4 + (x + dx) % 4

    def chip_from(dz, dx):
        return ((z + dz) % 2) * 4 + (x + 4 - dx) % 4

    g_copy = remote(gp.at[:, core], gp.at[:, core], misc.at[2], misc.at[3], dev_sib)
    g_copy.start()
    g_got = remote(gp.at[:, 1 - core], gp.at[:, 1 - core], misc.at[2], misc.at[3], dev_sib)

    def hr_copy(k):
        there = chip_to(*OTHERS[k])
        return remote(
            half_ref.at[:, :, pl.ds(pl.multiple_of(there * 128, 128), 128)],
            hrg.at[chip, :, pl.ds(0, 112)],
            hr_s.at[k], hr_r.at[k], {"chol": there * 2 + core},
        )

    def hr_got(k):
        ref = hrg.at[chip_from(*OTHERS[k]), :, pl.ds(0, 112)]
        return remote(ref, ref, hr_s.at[k], hr_r.at[k], dev_sib)

    for k in range(7):
        hr_copy(k).start()

    l_copy = remote(
        chol_ref.at[:, :, 1 - core], lst.at[pl.ds(2 * core, 2)], misc.at[4], misc.at[5], dev_sib
    )
    l_got = remote(
        lst.at[pl.ds(2 * (1 - core), 2)], lst.at[pl.ds(2 * (1 - core), 2)],
        misc.at[4], misc.at[5], dev_sib,
    )

    def s_copy(d, sending):
        there = (walk + d) % WALK if sending else (walk + WALK - d) % WALK
        return remote(
            stile, sall.at[walk] if sending else sall.at[there],
            w_s.at[d], w_r.at[d], {"walk": there},
        )

    def tiles(j):
        return pl.ds(SPANS[j][0], SPANS[j][1])

    def ag_send(ph, xg, j, k):
        ref = xg.at[tiles(j), chol]
        return remote(
            ref, ref, ag_s.at[ph, j, k], ag_r.at[ph, j, k],
            {"chol": chip_to(*OTHERS[k]) * 2 + core},
        )

    def ag_got(ph, xg, j, k):
        ref = xg.at[tiles(j), chip_from(*OTHERS[k]) * 2 + core]
        return remote(ref, ref, ag_s.at[ph, j, k], ag_r.at[ph, j, k], dev_sib)

    def sib(ph, xg, j, k, cc):
        there = chip if k == 7 else chip_from(*OTHERS[k])
        ref = xg.at[tiles(j), there * 2 + cc]
        return remote(ref, ref, sib_s.at[ph, j, k], sib_r.at[ph, j, k], dev_sib)

    def ag_start(ph, xg, j):
        for k in range(7):
            ag_send(ph, xg, j, k).start()
        sib(ph, xg, j, 7, core).start()

    def ag_relay(ph, xg, j):
        for k in reversed(range(7)):
            ag_got(ph, xg, j, k).wait_recv()
            sib(ph, xg, j, k, core).start()

    def ag_fin(ph, xg, j):
        for k in range(8):
            sib(ph, xg, j, k, 1 - core).wait_recv()

    def rs_copy(ph, j, k):
        there = chip_to(*OTHERS[k])
        return remote(
            part.at[ph, there, tiles(j)], got.at[ph, k, tiles(j)],
            rs_s.at[ph, j, k], rs_r.at[ph, j, k], {"chol": there * 2 + core},
        )

    def rs_start(ph, j):
        for k in range(7):
            rs_copy(ph, j, k).start()

    def rs_fin(ph, j):
        for k in range(7):
            rs_copy(ph, j, k).wait_recv()
        total = part[ph, chip, tiles(j)].astype(f32)
        for k in range(7):
            total = total + got[ph, k, tiles(j)].astype(f32)
        return total

    def matmul(ph, xg, j):
        start, size = SPANS[j]
        both = jnp.concatenate(
            [xg[start + n].reshape(1024, 128) for n in range(size)], axis=1
        )
        columns = pl.ds(0, 128 * size)
        for g in range(4):
            product = jnp.dot(
                lst[g].reshape(512, 1024), both, preferred_element_type=f32
            )
            scale = jnp.concatenate(
                [fb[g, pl.ds(start + n, 1), :] for n in range(size)], axis=1
            )
            if g == 0:
                acc[:, columns] = product * scale
            else:
                acc[:, columns] += product * scale
        for q in range(8):
            for n in range(size):
                part[ph, q, start + n] = acc[
                    pl.ds(64 * q, 64), pl.ds(128 * n, 128)
                ].astype(bf16)

    for j in range(CHUNKS):
        ag_start(0, xg1, j)
    l_copy.start()

    @pl.loop(1, WALK)
    def _(d):
        s_copy(d, True).start()

    for load in loads[3:]:
        load.wait()
    own_h.wait()
    g_got.wait_recv()
    for k in range(7):
        hr_got(k).wait_recv()

    eye = (
        lax.broadcasted_iota(jnp.int32, (128, 128), 0)
        == lax.broadcasted_iota(jnp.int32, (128, 128), 1)
    ).astype(f32)
    greens = gp[...].reshape(1024, 128)

    def one_vector(v, tile):
        source, which = v // 2, v % 2
        product = jnp.dot(greens, hrg[source, which], preferred_element_type=f32)
        picked = jnp.sum(product.reshape(8, 128, 128) * eye[None], axis=1)
        value = jnp.sum(picked, axis=1, keepdims=True)
        return jnp.where(lane8 == source * 4 + core * 2 + which, field_scale * value, tile)

    tile = lax.fori_loop(0, 16, one_vector, jnp.zeros((8, 128), f32))
    for which in range(2):
        shift = mean_in[index_in[which]]
        for w in range(8):
            tile = tile + jnp.where(
                (row8 == w) & (lane8 == chol * 2 + which),
                noise_in[which, w] - field_scale * shift, 0.0,
            )
    btile[chol] = tile

    def b_copy(d, sending):
        there = (chol + d) % 16 if sending else (chol + 16 - d) % 16
        slot = chol if sending else there
        return remote(
            btile.at[slot], btile.at[slot], b_s.at[d], b_r.at[d], {"chol": there}
        )

    @pl.loop(1, 16)
    def _(d):
        b_copy(d, True).start()

    ag_relay(0, xg1, 0)

    @pl.loop(1, WALK)
    def _(d):
        s_copy(d, False).wait_recv()

    low = sall[...]
    wanted = jnp.stack([low, low + 8], axis=1).reshape(WALK * 16, 128)
    wide = lax.broadcasted_iota(jnp.int32, (WALK * 16, 128), 1)
    for b in range(4):
        picks[b] = jnp.where(wanted == wide + 128 * b, 1.0, 0.0).astype(bf16)

    ag_relay(0, xg1, 1)

    @pl.loop(1, 16)
    def _(d):
        b_copy(d, False).wait_recv()

    field = btile[0]
    for c in range(1, 16):
        field = field + btile[c]
    for g in range(4):
        value = jnp.sum(
            jnp.where(lane8 == chip * 4 + g, field, 0.0), axis=1, keepdims=True
        )
        for t in range(TILES):
            column = lane8 + 128 * t
            mine = (column >= OCC * row8) & (column < OCC * (row8 + 1))
            fb[g, pl.ds(t, 1), :] = jnp.sum(
                jnp.where(mine, value, 0.0), axis=0, keepdims=True
            )

    own_l.wait()
    l_got.wait_recv()

    def mm1(j):
        ag_fin(0, xg1, j)
        matmul(0, xg1, j)
        rs_start(0, j)

    def turn(j):
        term = field_scale * rs_fin(0, j)
        first[tiles(j)] = term
        xg2[tiles(j), chol] = term.astype(bf16)
        ag_start(1, xg2, j)

    def mm2(j):
        ag_fin(1, xg2, j)
        matmul(1, xg2, j)
        rs_start(1, j)

    def finish(j):
        done_tiles = (
            xg1[tiles(j), chol].astype(f32)
            + first[tiles(j)]
            + (0.5 * field_scale) * rs_fin(1, j)
        )
        first[tiles(j)] = done_tiles

    mm1(0)
    ag_relay(0, xg1, 2)
    mm1(1)
    ag_relay(0, xg1, 3)
    turn(0)
    mm1(2)
    turn(1)
    mm1(3)
    ag_relay(1, xg2, 0)
    turn(2)
    ag_relay(1, xg2, 1)
    mm2(0)
    turn(3)
    ag_relay(1, xg2, 2)
    mm2(1)
    ag_relay(1, xg2, 3)
    finish(0)
    mm2(2)
    finish(1)
    mm2(3)
    finish(2)
    finish(3)

    for w in range(8):
        t, start = (OCC * w) // 128, (OCC * w) % 128
        if start:
            mixed = jnp.where(lanes >= start, first[t], first[min(t + 1, TILES - 1)])
            mixed = pltpu.roll(mixed, 128 - start, 1)
        else:
            mixed = first[t]
        final[pl.ds(64 * w, 64)] = mixed

    for p in range(WALK):
        zsend[p] = jnp.concatenate(
            [final[pl.ds(2 * p, 8, stride=64), :], final[pl.ds(2 * p + 1, 8, stride=64), :]],
            axis=0,
        ).astype(bf16)
    zrecv[walk] = zsend[walk]

    def z_copy(d, sending):
        there = (walk + d) % WALK if sending else (walk + WALK - d) % WALK
        return remote(
            zsend.at[there], zrecv.at[walk] if sending else zrecv.at[there],
            z_s.at[d], z_r.at[d], {"walk": there},
        )

    def y_copy(d, sending):
        there = (walk + d) % WALK if sending else (walk + WALK - d) % WALK
        return remote(
            ysend.at[there], yrecv.at[walk] if sending else yrecv.at[there],
            y_s.at[d], y_r.at[d], {"walk": there},
        )

    @pl.loop(1, WALK)
    def _(d):
        z_copy(d, True).start()

    @pl.loop(1, WALK)
    def _(d):
        z_copy(d, False).wait_recv()

    here = zrecv[...].reshape(WALK * 16, 128)
    taken = jnp.dot(picks[0], here[0:128], preferred_element_type=f32)
    for b in range(1, 4):
        taken = taken + jnp.dot(
            picks[b], here[128 * b : 128 * (b + 1)], preferred_element_type=f32
        )
    ysend[...] = taken.astype(bf16).reshape(WALK, 16, 128)
    yrecv[walk] = ysend[walk]

    @pl.loop(1, WALK)
    def _(d):
        y_copy(d, True).start()

    g_copy.wait_send()
    l_copy.wait_send()
    for k in range(7):
        hr_copy(k).wait_send()

    @pl.loop(1, 16)
    def _(d):
        b_copy(d, True).wait_send()

    for ph, xg in ((0, xg1), (1, xg2)):
        for j in range(CHUNKS):
            for k in range(7):
                ag_send(ph, xg, j, k).wait_send()
                rs_copy(ph, j, k).wait_send()
            for k in range(8):
                sib(ph, xg, j, k, core).wait_send()

    @pl.loop(1, WALK)
    def _(d):
        s_copy(d, True).wait_send()
        z_copy(d, True).wait_send()

    @pl.loop(1, WALK)
    def _(d):
        y_copy(d, False).wait_recv()

    for p in range(WALK):
        both = yrecv[p].astype(f32)
        final[pl.ds(2 * p, 8, stride=64), :] = both[0:8]
        final[pl.ds(2 * p + 1, 8, stride=64), :] = both[8:16]
    out_ref[...] = final[...].reshape(8, 64, 128)[:, :, 0:OCC].astype(bf16)

    @pl.loop(1, WALK)
    def _(d):
        y_copy(d, True).wait_send()


def per_device(
    cholesky, half_rotated, green_half, walker, aux_noise, mf_shift, chol_index, walker_source
):
    bf16, f32, i32 = jnp.bfloat16, jnp.float32, jnp.int32
    V, S, D = pltpu.VMEM, pltpu.SMEM, pltpu.SemaphoreType.DMA
    moved = pl.pallas_call(
        body,
        out_shape=jax.ShapeDtypeStruct((8, 64, OCC), bf16),
        in_specs=[pl.BlockSpec(memory_space=pltpu.HBM)] * 8,
        out_specs=pl.BlockSpec(memory_space=pltpu.VMEM),
        scratch_shapes=[
            V((4, 8, 64, 1024), bf16),
            V((TILES, 16, 64, 128), bf16),
            V((TILES, 16, 64, 128), bf16),
            V((2, 8, TILES, 64, 128), bf16),
            V((2, 7, TILES, 64, 128), bf16),
            V((TILES, 64, 128), f32),
            V((512, 256), f32),
            V((8, 2, 128, 128), bf16),
            V((8, 2, 64, 128), bf16),
            V((4, 8, 128), f32),
            V((16, 8, 128), f32),
            V((8, 64, 128), f32),
            V((512, 128), f32),
            V((WALK, 16, 128), bf16),
            V((WALK, 16, 128), bf16),
            V((WALK, 16, 128), bf16),
            V((WALK, 16, 128), bf16),
            V((8, 128), i32),
            V((WALK, 8, 128), i32),
            V((4, WALK * 16, 128), bf16),
            V((8, 64, OCC), bf16),
            V((8, 64, OCC), bf16),
            S((2, 8), f32),
            S((4000,), f32),
            S((2,), i32),
            S((8,), i32),
            D((2, CHUNKS, 7)),
            D((2, CHUNKS, 7)),
            D((2, CHUNKS, 8)),
            D((2, CHUNKS, 8)),
            D((2, CHUNKS, 7)),
            D((2, CHUNKS, 7)),
            D((7,)),
            D((7,)),
            D((16,)),
            D((16,)),
            D((WALK,)),
            D((WALK,)),
            D((WALK,)),
            D((WALK,)),
            D((WALK,)),
            D((WALK,)),
            D((6,)),
            D((6,)),
        ],
        compiler_params=pltpu.CompilerParams(
            collective_id=0, has_side_effects=True, vmem_limit_bytes=48 * 1024 * 1024
        ),
        cost_estimate=pl.CostEstimate(
            flops=8_600_000_000, bytes_accessed=6_000_000, transcendentals=0
        ),
    )(
        cholesky.reshape(2, 8, 2, 64, 1024),
        jnp.pad(half_rotated, ((0, 0), (0, 12), (0, 0))),
        jnp.transpose(green_half, (0, 2, 1)),
        jnp.transpose(walker, (0, 2, 1)),
        jnp.transpose(aux_noise, (1, 0)),
        mf_shift,
        chol_index,
        walker_source,
    )
    return jnp.transpose(moved, (0, 2, 1))


def solution(mesh):
    placed = (
        P("chol", None, None),
        P("chol", None, None),
        P("walk", None, "chol"),
        P("walk", None, "chol"),
        P("walk", "chol"),
        P(),
        P("chol"),
        P("walk"),
    )
    return jax.shard_map(
        per_device, mesh=mesh, in_specs=placed, out_specs=P("walk", None, "chol"), check_vma=False
    )
```

time: 405 us -> 104 us (0.26)
  waiting for transfers between devices: 358 us -> 0 us
  Pallas kernels: 0 us -> 93.5 us
  matrix products: 19.2 us -> 0 us
  between operations: 13.6 us -> 0.04 us
  other arithmetic: 4.92 us -> 0 us
    all_gather x4 -> x0, waiting for transfers between devices: 226 us -> none  [the longest x1 104 us: per_device(): everyone = lax.all_gather(propagated, 'walk', axis=0, tiled=True)]
    reduce_scatter x2 -> x0, waiting for transfers between devices: 131 us -> none  [the longest x1 65.6 us: per_device(): lax.psum_scatter(propagate(walker_all).astype(jnp.bfloat16), 'chol', scat...]
    pallas_call x0 -> x1, Pallas kernels: none -> 93.5 us  [per_device(): pl.pallas_call(body, out_shape=jax.ShapeDtypeStruct((8, 64, OCC), bf16),...]
    dot_general x5 -> x0, matrix products: 19.2 us -> none  [the longest x4 17.9 us: propagate(): lax.dot_general(flat_rows, cholesky[vector], (((1,), (1,)), ((), ())), pr...]
    unnamed x19 -> x16, local copies, waits for them, and re-layouts: 1.73 us -> 8.43 us
  transfers between devices with their start and end apart: 6 -> 0, of which waited for: 6 -> 0; matrix products, arithmetic and copies ran while one was open for 1% -> 0% of each run, Pallas kernels for 0% -> 0%
where the time goes in v2:
time: 104 us; the launch traced here: 102 us
  Pallas kernels  93.5 us (90%)
  local copies, waits for them, and re-layouts  8.47 us (8%)
    pallas_call x1, Pallas kernels, per_device(): pl.pallas_call(body, out_shape=jax.ShapeDtypeStruct((8, 64, OCC), bf16),...  93.5 us
    unnamed x16, local copies, waits for them, and re-layouts  8.43 us

profile of v2, /device:TPU:1, one launch (start us, length us, event | category | flops | bytes accessed | tf_op | source)
XLA Modules:
  0.0 102.0 jit_solution(13171778690905643806)
XLA Ops:
  0.0 1.1 %copy.9 = bf16[2,100,1024]{2,1,0:T(8,128)(2,1)S(1)} copy(bf16[2,100,1024]{2,0,1:T(2,128)(2,1)} %param.9) | data formatting | bytes 819200 | tf_op args[1]
  1.1 0.0 copy-start
  1.1 2.2 %copy-done = bf16[2,1024,1024]{2,1,0:T(8,128)(2,1)S(1)} copy-done((bf16[2,1024,1024]{2,1,0:T(8,128)(2,1)S(1)}, bf16[2,1024,1024]{2,1,0:T(8,128)(2,1)}, u32[]{:S(2)}) %copy-start) | copy-done | bytes 4194328
  3.3 0.0 copy-start.1
  3.3 0.9 copy-done.1
  4.2 0.0 copy-start.2
  4.2 0.9 copy-done.2
  5.1 0.0 copy-start.3
  5.1 0.7 copy-done.3
  5.9 0.0 copy-start.4
  5.9 0.7 copy-done.4
  6.5 0.0 copy-start.5
  6.5 0.7 copy-done.5
  7.2 0.0 copy-start.6
  7.2 0.7 copy-done.6
  7.8 93.5 %shard_map.82 = bf16[8,64,100]{2,1,0:T(8,128)(2,1)S(1)} custom-call(bf16[2,8,2,64,1024]{4,3,2,1,0:T(8,128)(2,1)S(1)} %bitcast.6, bf16[2,112,1024]{2,1,0:T(8,128)(2,1)S(1)} %pad.4.half_ref, bf16[8,64,100]{2,1,0:T(8,128)(2,1)S(1)} %bitcast.7, bf16[8,64,100]{2,1,0:T(8,128)(2,1)S(1)} %bitcast.8, f32[2,8]{1,0:T(2,128)S(1)} %bitcast.9, f32[4000]{0:T(1024)S(1)} %copy-done.3, ...), custom_call_target="tpu_custom_call" | custom-call | flops 8600000512 | bytes 6000000 | tf_op jit(solution)/shard_map/pallas_call | solution.py:448
  101.4 0.7 copy.11
  (1 shorter events, 0.0 us)
Async XLA Ops:
  1.1 2.2 %copy-start = (bf16[2,1024,1024]{2,1,0:T(8,128)(2,1)S(1)}, bf16[2,1024,1024]{2,1,0:T(8,128)(2,1)}, u32[]{:S(2)}) copy-start(bf16[2,1024,1024]{2,1,0:T(8,128)(2,1)} %param.8) | copy-start | bytes 12582916
  3.3 0.9 copy-start.1
  4.2 0.9 copy-start.2
  5.1 0.7 copy-start.3
  5.9 0.7 copy-start.4
  6.5 0.7 copy-start.5
  7.2 0.7 copy-start.6

commit v3 on v2

--- a/solution.py
+++ b/solution.py
@@ -18,10 +18,10 @@
 def body(
     chol_ref, half_ref, green_ref, walker_ref, noise_ref, mean_ref, index_ref, source_ref,
     out_ref,
-    lst, xg1, xg2, part, got, first, acc, hrg, gp, fb, btile, done, final,
-    zsend, zrecv, ysend, yrecv, stile, sall, picks,
+    lst, xg1, xg2, part, got, first, acc, hrg, gp, fb, btile, final,
+    zsend, zrecv, ysend, yrecv, stile, sall, fall, fsel,
     green_in, walker_in, noise_in, mean_in, index_in, source_in,
-    ag_s, ag_r, sib_s, sib_r, rs_s, rs_r, hr_s, hr_r, b_s, b_r, w_s, w_r, z_s, z_r, y_s, y_r,
+    ag_s, ag_r, sib_s, sib_r, rs_s, rs_r, hr_s, hr_r, b_s, b_r, w_s, w_r, z_s, z_r, y_s, y_r, f_s, f_r,
     misc, in_sem,
 ):
     f32, bf16 = jnp.float32, jnp.bfloat16
@@ -81,19 +81,14 @@
     sall[walk] = ids
 
     loads[1].wait()
-    done[...] = jnp.zeros_like(done)
-    done[:, :, 0:OCC] = walker_in[...].astype(f32)
-    lanes = lax.broadcasted_iota(jnp.int32, (64, 128), 1)
-    shifted = [
-        pltpu.roll(done[w], (OCC * w) % 128, 1) if w else done[w] for w in range(8)
-    ]
-    for t in range(TILES):
-        tile = jnp.zeros((64, 128), f32)
-        for w in range(8):
-            low, high = OCC * w - 128 * t, OCC * (w + 1) - 128 * t
-            if high > 0 and low < 128:
-                tile = jnp.where((lanes >= low) & (lanes < high), shifted[w], tile)
-        xg1[t, chol] = tile.astype(bf16)
+    final[...] = jnp.zeros_like(final)
+    final[:, 0:OCC] = walker_in[...].astype(f32).reshape(512, OCC)
+    for p in range(WALK):
+        zsend[p] = jnp.concatenate(
+            [final[pl.ds(2 * p, 8, stride=64), :], final[pl.ds(2 * p + 1, 8, stride=64), :]],
+            axis=0,
+        ).astype(bf16)
+    zrecv[walk] = zsend[walk]
     loads[2].wait()
     gp[:, core] = jnp.zeros((8, 64, 128), bf16)
     gp[:, core, :, 0:OCC] = green_in[...]
@@ -111,6 +106,37 @@
 
     def chip_from(dz, dx):
         return ((z + dz) % 2) * 4 + (x + 4 - dx) % 4
+
+    def walk_peer(d, sending):
+        return (walk + d) % WALK if sending else (walk + WALK - d) % WALK
+
+    def walk_copy(src, dst, ssem, rsem, d, sending):
+        there = walk_peer(d, sending)
+        return remote(src, dst, ssem.at[d], rsem.at[d], {"walk": there})
+
+    def s_copy(d, sending):
+        slot = walk if sending else walk_peer(d, sending)
+        return walk_copy(stile, sall.at[slot], w_s, w_r, d, sending)
+
+    def z_copy(d, sending):
+        there = walk_peer(d, sending)
+        slot = walk if sending else there
+        return walk_copy(zsend.at[there], zrecv.at[slot], z_s, z_r, d, sending)
+
+    def y_copy(d, sending):
+        there = walk_peer(d, sending)
+        slot = walk if sending else there
+        return walk_copy(ysend.at[there], yrecv.at[slot], y_s, y_r, d, sending)
+
+    def f_copy(d, sending):
+        slot = walk if sending else walk_peer(d, sending)
+        ref = fall.at[pl.ds(pl.multiple_of(8 * slot, 8), 8)]
+        return walk_copy(ref, ref, f_s, f_r, d, sending)
+
+    @pl.loop(1, WALK)
+    def _(d):
+        z_copy(d, True).start()
+        s_copy(d, True).start()
 
     g_copy = remote(gp.at[:, core], gp.at[:, core], misc.at[2], misc.at[3], dev_sib)
     g_copy.start()
@@ -138,13 +164,6 @@
         lst.at[pl.ds(2 * (1 - core), 2)], lst.at[pl.ds(2 * (1 - core), 2)],
         misc.at[4], misc.at[5], dev_sib,
     )
-
-    def s_copy(d, sending):
-        there = (walk + d) % WALK if sending else (walk + WALK - d) % WALK
-        return remote(
-            stile, sall.at[walk] if sending else sall.at[there],
-            w_s.at[d], w_r.at[d], {"walk": there},
-        )
 
     def tiles(j):
         return pl.ds(SPANS[j][0], SPANS[j][1])
@@ -221,13 +240,33 @@
                     pl.ds(64 * q, 64), pl.ds(128 * n, 128)
                 ].astype(bf16)
 
-    for j in range(CHUNKS):
-        ag_start(0, xg1, j)
     l_copy.start()
 
     @pl.loop(1, WALK)
     def _(d):
-        s_copy(d, True).start()
+        s_copy(d, False).wait_recv()
+
+    low = sall[...]
+    wanted = jnp.stack([low, low + 8], axis=1).reshape(WALK * 16, 128)
+    wide = lax.broadcasted_iota(jnp.int32, (WALK * 16, 128), 1)
+    picks = [jnp.where(wanted == wide + 128 * b, 1.0, 0.0).astype(bf16) for b in range(4)]
+
+    @pl.loop(1, WALK)
+    def _(d):
+        z_copy(d, False).wait_recv()
+
+    here = zrecv[...].reshape(WALK * 16, 128)
+    taken = jnp.dot(picks[0], here[0:128], preferred_element_type=f32)
+    for b in range(1, 4):
+        taken = taken + jnp.dot(
+            picks[b], here[128 * b : 128 * (b + 1)], preferred_element_type=f32
+        )
+    ysend[...] = taken.astype(bf16).reshape(WALK, 16, 128)
+    yrecv[walk] = ysend[walk]
+
+    @pl.loop(1, WALK)
+    def _(d):
+        y_copy(d, True).start()
 
     for load in loads[3:]:
         load.wait()
@@ -270,20 +309,6 @@
     def _(d):
         b_copy(d, True).start()
 
-    ag_relay(0, xg1, 0)
-
-    @pl.loop(1, WALK)
-    def _(d):
-        s_copy(d, False).wait_recv()
-
-    low = sall[...]
-    wanted = jnp.stack([low, low + 8], axis=1).reshape(WALK * 16, 128)
-    wide = lax.broadcasted_iota(jnp.int32, (WALK * 16, 128), 1)
-    for b in range(4):
-        picks[b] = jnp.where(wanted == wide + 128 * b, 1.0, 0.0).astype(bf16)
-
-    ag_relay(0, xg1, 1)
-
     @pl.loop(1, 16)
     def _(d):
         b_copy(d, False).wait_recv()
@@ -291,6 +316,44 @@
     field = btile[0]
     for c in range(1, 16):
         field = field + btile[c]
+    fall[pl.ds(pl.multiple_of(8 * walk, 8), 8)] = field
+
+    @pl.loop(1, WALK)
+    def _(d):
+        f_copy(d, True).start()
+
+    @pl.loop(1, WALK)
+    def _(d):
+        y_copy(d, False).wait_recv()
+
+    for p in range(WALK):
+        both = yrecv[p].astype(f32)
+        final[pl.ds(2 * p, 8, stride=64), :] = both[0:8]
+        final[pl.ds(2 * p + 1, 8, stride=64), :] = both[8:16]
+    lanes = lax.broadcasted_iota(jnp.int32, (64, 128), 1)
+    shifted = [final[pl.ds(64 * w, 64)] for w in range(8)]
+    shifted = [
+        pltpu.roll(v, (OCC * w) % 128, 1) if w else v for w, v in enumerate(shifted)
+    ]
+    for t in range(TILES):
+        tile = jnp.zeros((64, 128), f32)
+        for w in range(8):
+            left, right = OCC * w - 128 * t, OCC * (w + 1) - 128 * t
+            if right > 0 and left < 128:
+                tile = jnp.where((lanes >= left) & (lanes < right), shifted[w], tile)
+        xg1[t, chol] = tile.astype(bf16)
+    for j in range(CHUNKS):
+        ag_start(0, xg1, j)
+
+    ag_relay(0, xg1, 0)
+
+    @pl.loop(1, WALK)
+    def _(d):
+        f_copy(d, False).wait_recv()
+
+    for s in range(8):
+        fsel[pl.ds(s, 1), :] = fall[pl.ds(source_in[s], 1), :]
+    field = fsel[...]
     for g in range(4):
         value = jnp.sum(
             jnp.where(lane8 == chip * 4 + g, field, 0.0), axis=1, keepdims=True
@@ -302,6 +365,7 @@
                 jnp.where(mine, value, 0.0), axis=0, keepdims=True
             )
 
+    ag_relay(0, xg1, 1)
     own_l.wait()
     l_got.wait_recv()
 
@@ -359,49 +423,7 @@
             mixed = pltpu.roll(mixed, 128 - start, 1)
         else:
             mixed = first[t]
-        final[pl.ds(64 * w, 64)] = mixed
-
-    for p in range(WALK):
-        zsend[p] = jnp.concatenate(
-            [final[pl.ds(2 * p, 8, stride=64), :], final[pl.ds(2 * p + 1, 8, stride=64), :]],
-            axis=0,
-        ).astype(bf16)
-    zrecv[walk] = zsend[walk]
-
-    def z_copy(d, sending):
-        there = (walk + d) % WALK if sending else (walk + WALK - d) % WALK
-        return remote(
-            zsend.at[there], zrecv.at[walk] if sending else zrecv.at[there],
-            z_s.at[d], z_r.at[d], {"walk": there},
-        )
-
-    def y_copy(d, sending):
-        there = (walk + d) % WALK if sending else (walk + WALK - d) % WALK
-        return remote(
-            ysend.at[there], yrecv.at[walk] if sending else yrecv.at[there],
-            y_s.at[d], y_r.at[d], {"walk": there},
-        )
-
-    @pl.loop(1, WALK)
-    def _(d):
-        z_copy(d, True).start()
-
-    @pl.loop(1, WALK)
-    def _(d):
-        z_copy(d, False).wait_recv()
-
-    here = zrecv[...].reshape(WALK * 16, 128)
-    taken = jnp.dot(picks[0], here[0:128], preferred_element_type=f32)
-    for b in range(1, 4):
-        taken = taken + jnp.dot(
-            picks[b], here[128 * b : 128 * (b + 1)], preferred_element_type=f32
-        )
-    ysend[...] = taken.astype(bf16).reshape(WALK, 16, 128)
-    yrecv[walk] = ysend[walk]
-
-    @pl.loop(1, WALK)
-    def _(d):
-        y_copy(d, True).start()
+        out_ref[w] = mixed[:, 0:OCC].astype(bf16)
 
     g_copy.wait_send()
     l_copy.wait_send()
@@ -424,20 +446,8 @@
     def _(d):
         s_copy(d, True).wait_send()
         z_copy(d, True).wait_send()
-
-    @pl.loop(1, WALK)
-    def _(d):
-        y_copy(d, False).wait_recv()
-
-    for p in range(WALK):
-        both = yrecv[p].astype(f32)
-        final[pl.ds(2 * p, 8, stride=64), :] = both[0:8]
-        final[pl.ds(2 * p + 1, 8, stride=64), :] = both[8:16]
-    out_ref[...] = final[...].reshape(8, 64, 128)[:, :, 0:OCC].astype(bf16)
-
-    @pl.loop(1, WALK)
-    def _(d):
         y_copy(d, True).wait_send()
+        f_copy(d, True).wait_send()
 
 
 def per_device(
@@ -462,7 +472,6 @@
             V((8, 2, 64, 128), bf16),
             V((4, 8, 128), f32),
             V((16, 8, 128), f32),
-            V((8, 64, 128), f32),
             V((512, 128), f32),
             V((WALK, 16, 128), bf16),
             V((WALK, 16, 128), bf16),
@@ -470,7 +479,8 @@
             V((WALK, 16, 128), bf16),
             V((8, 128), i32),
             V((WALK, 8, 128), i32),
-            V((4, WALK * 16, 128), bf16),
+            V((256, 128), f32),
+            V((8, 128), f32),
             V((8, 64, OCC), bf16),
             V((8, 64, OCC), bf16),
             S((2, 8), f32),
@@ -493,11 +503,13 @@
             D((WALK,)),
             D((WALK,)),
             D((WALK,)),
+            D((WALK,)),
+            D((WALK,)),
             D((6,)),
             D((6,)),
         ],
         compiler_params=pltpu.CompilerParams(
-            collective_id=0, has_side_effects=True, vmem_limit_bytes=48 * 1024 * 1024
+            collective_id=0, has_side_effects=True, vmem_limit_bytes=64 * 1024 * 1024
         ),
         cost_estimate=pl.CostEstimate(
             flops=8_600_000_000, bytes_accessed=6_000_000, transcendentals=0

time: 104 us -> 96.7 us (0.930); the launches traced: 102 us -> 96.5 us
  local copies, waits for them, and re-layouts: 8.47 us -> 3.46 us
    unnamed x16 -> x2, local copies, waits for them, and re-layouts: 8.43 us -> 2.65 us
where the time goes in v3:
time: 96.7 us; the launch traced here: 96.5 us
  Pallas kernels  93 us (96%)
  local copies, waits for them, and re-layouts  3.46 us (4%)
    pallas_call x1, Pallas kernels, per_device(): pl.pallas_call(body, out_shape=jax.ShapeDtypeStruct((8, 64, OCC), bf16),...  93 us
    unnamed x2, local copies, waits for them, and re-layouts  2.65 us

profile of v3, /device:TPU:1, one launch (start us, length us, event | category | flops | bytes accessed | tf_op | source)
XLA Modules:
  0.0 96.5 jit_solution(14920783895603426895)
XLA Ops:
  0.0 1.1 %copy.9 = bf16[2,100,1024]{2,1,0:T(8,128)(2,1)S(1)} copy(bf16[2,100,1024]{2,0,1:T(2,128)(2,1)} %param.9) | data formatting | bytes 819200 | tf_op args[1]
  1.1 0.8 pad.4.half_ref
  1.9 93.0 %shard_map.82 = bf16[8,64,100]{2,1,0:T(8,128)(2,1)} custom-call(bf16[2,8,2,64,1024]{4,3,2,1,0:T(8,128)(2,1)} %bitcast.6, bf16[2,112,1024]{2,1,0:T(8,128)(2,1)} %pad.4.half_ref, bf16[8,64,100]{2,1,0:T(8,128)(2,1)} %bitcast.7, bf16[8,64,100]{2,1,0:T(8,128)(2,1)} %bitcast.8, f32[2,8]{1,0:T(2,128)} %bitcast.9, f32[4000]{0:T(1024)} %mean_ref.1, s32[2]{0:T(128)} %index_ref.1, ...), custom_call_target="tpu_custom_call" | custom-call | flops 8600000512 | bytes 6000000 | tf_op jit(solution)/shard_map/pallas_call | solution.py:458
  94.9 1.6 %copy.11 = bf16[8,100,64]{1,2,0:T(8,128)(2,1)} copy(bf16[8,100,64]{1,2,0:T(8,128)(2,1)} %bitcast.5) | data formatting | bytes 204800

commit v4 on v3

--- a/solution.py
+++ b/solution.py
@@ -73,12 +73,13 @@
     row8 = lax.broadcasted_iota(jnp.int32, (8, 128), 0)
     lane8 = lax.broadcasted_iota(jnp.int32, (8, 128), 1)
     loads[0].wait()
-    ids = jnp.zeros((8, 128), jnp.int32)
+    lane1 = lax.broadcasted_iota(jnp.int32, (1, 128), 1)
+    ids = jnp.zeros((1, 128), jnp.int32)
     for s in range(8):
         value = source_in[s]
-        ids = jnp.where(row8 == s, (value // 8) * 16 + value % 8, ids)
-    stile[...] = ids
-    sall[walk] = ids
+        ids = jnp.where(lane1 == s, (value // 8) * 16 + value % 8, ids)
+    stile[...] = ids.astype(f32)
+    sall[walk] = ids.astype(f32)
 
     loads[1].wait()
     final[...] = jnp.zeros_like(final)
@@ -246,9 +247,12 @@
     def _(d):
         s_copy(d, False).wait_recv()
 
-    low = sall[...]
+    low = jnp.sum(
+        jnp.where((lane8 == row8)[None], sall[...], 0.0), axis=2, keepdims=True
+    )
+    low = jnp.broadcast_to(low, (WALK, 8, 128))
     wanted = jnp.stack([low, low + 8], axis=1).reshape(WALK * 16, 128)
-    wide = lax.broadcasted_iota(jnp.int32, (WALK * 16, 128), 1)
+    wide = lax.broadcasted_iota(jnp.int32, (WALK * 16, 128), 1).astype(f32)
     picks = [jnp.where(wanted == wide + 128 * b, 1.0, 0.0).astype(bf16) for b in range(4)]
 
     @pl.loop(1, WALK)
@@ -275,20 +279,30 @@
     for k in range(7):
         hr_got(k).wait_recv()
 
-    eye = (
-        lax.broadcasted_iota(jnp.int32, (128, 128), 0)
-        == lax.broadcasted_iota(jnp.int32, (128, 128), 1)
+    same = (
+        lax.broadcasted_iota(jnp.int32, (64, 128), 0)
+        == lax.broadcasted_iota(jnp.int32, (64, 128), 1) % 64
     ).astype(f32)
-    greens = gp[...].reshape(1024, 128)
-
-    def one_vector(v, tile):
-        source, which = v // 2, v % 2
-        product = jnp.dot(greens, hrg[source, which], preferred_element_type=f32)
-        picked = jnp.sum(product.reshape(8, 128, 128) * eye[None], axis=1)
-        value = jnp.sum(picked, axis=1, keepdims=True)
-        return jnp.where(lane8 == source * 4 + core * 2 + which, field_scale * value, tile)
-
-    tile = lax.fori_loop(0, 16, one_vector, jnp.zeros((8, 128), f32))
+
+    def one_source(source, tile):
+        pair = (hrg[source, 0], hrg[source, 1])
+        picked = jnp.zeros((8, 128), f32)
+        for half in range(2):
+            columns = jnp.concatenate([h[:, 64 * half : 64 * half + 64] for h in pair], axis=1)
+            product = jnp.dot(
+                gp[:, half].reshape(512, 128), columns, preferred_element_type=f32
+            )
+            picked = picked + jnp.sum(product.reshape(8, 64, 128) * same[None], axis=1)
+        for which in range(2):
+            value = jnp.sum(
+                jnp.where((lane8 >= 64) == bool(which), picked, 0.0), axis=1, keepdims=True
+            )
+            tile = jnp.where(
+                lane8 == source * 4 + core * 2 + which, field_scale * value, tile
+            )
+        return tile
+
+    tile = lax.fori_loop(0, 8, one_source, jnp.zeros((8, 128), f32))
     for which in range(2):
         shift = mean_in[index_in[which]]
         for w in range(8):
@@ -308,19 +322,6 @@
     @pl.loop(1, 16)
     def _(d):
         b_copy(d, True).start()
-
-    @pl.loop(1, 16)
-    def _(d):
-        b_copy(d, False).wait_recv()
-
-    field = btile[0]
-    for c in range(1, 16):
-        field = field + btile[c]
-    fall[pl.ds(pl.multiple_of(8 * walk, 8), 8)] = field
-
-    @pl.loop(1, WALK)
-    def _(d):
-        f_copy(d, True).start()
 
     @pl.loop(1, WALK)
     def _(d):
@@ -344,6 +345,19 @@
         xg1[t, chol] = tile.astype(bf16)
     for j in range(CHUNKS):
         ag_start(0, xg1, j)
+
+    @pl.loop(1, 16)
+    def _(d):
+        b_copy(d, False).wait_recv()
+
+    field = btile[0]
+    for c in range(1, 16):
+        field = field + btile[c]
+    fall[pl.ds(pl.multiple_of(8 * walk, 8), 8)] = field
+
+    @pl.loop(1, WALK)
+    def _(d):
+        f_copy(d, True).start()
 
     ag_relay(0, xg1, 0)
 
@@ -477,8 +491,8 @@
             V((WALK, 16, 128), bf16),
             V((WALK, 16, 128), bf16),
             V((WALK, 16, 128), bf16),
-            V((8, 128), i32),
-            V((WALK, 8, 128), i32),
+            V((1, 128), f32),
+            V((WALK, 1, 128), f32),
             V((256, 128), f32),
             V((8, 128), f32),
             V((8, 64, OCC), bf16),

time: 96.7 us -> 93.3 us (0.965)
  Pallas kernels: 93 us -> 89.7 us
    pallas_call x1, Pallas kernels: 93 us -> 89.7 us  [per_device(): pl.pallas_call(body, out_shape=jax.ShapeDtypeStruct((8, 64, OCC), bf16),...]
where the time goes in v4:
time: 93.3 us; the launch traced here: 93.2 us
  Pallas kernels  89.7 us (96%)
  local copies, waits for them, and re-layouts  3.46 us (4%)
    pallas_call x1, Pallas kernels, per_device(): pl.pallas_call(body, out_shape=jax.ShapeDtypeStruct((8, 64, OCC), bf16),...  89.7 us
    unnamed x2, local copies, waits for them, and re-layouts  2.65 us

profile of v4, /device:TPU:1, one launch (start us, length us, event | category | flops | bytes accessed | tf_op | source)
XLA Modules:
  0.0 93.2 jit_solution(15514103745163709014)
XLA Ops:
  0.0 1.1 %copy.9 = bf16[2,100,1024]{2,1,0:T(8,128)(2,1)S(1)} copy(bf16[2,100,1024]{2,0,1:T(2,128)(2,1)} %param.9) | data formatting | bytes 819200 | tf_op args[1]
  1.1 0.8 pad.4.half_ref
  1.9 89.7 %shard_map.82 = bf16[8,64,100]{2,1,0:T(8,128)(2,1)} custom-call(bf16[2,8,2,64,1024]{4,3,2,1,0:T(8,128)(2,1)} %bitcast.6, bf16[2,112,1024]{2,1,0:T(8,128)(2,1)} %pad.4.half_ref, bf16[8,64,100]{2,1,0:T(8,128)(2,1)} %bitcast.7, bf16[8,64,100]{2,1,0:T(8,128)(2,1)} %bitcast.8, f32[2,8]{1,0:T(2,128)} %bitcast.9, f32[4000]{0:T(1024)} %mean_ref.1, s32[2]{0:T(128)} %index_ref.1, ...), custom_call_target="tpu_custom_call" | custom-call | flops 8600000512 | bytes 6000000 | tf_op jit(solution)/shard_map/pallas_call | solution.py:472
  91.6 1.6 %copy.11 = bf16[8,100,64]{1,2,0:T(8,128)(2,1)} copy(bf16[8,100,64]{1,2,0:T(8,128)(2,1)} %bitcast.5) | data formatting | bytes 204800

commit v5 on v4

--- a/solution.py
+++ b/solution.py
@@ -8,7 +8,7 @@
 MESH = pl.DeviceIdType.MESH
 field_scale = 0.1
 TILES = 7
-SPANS = ((0, 2), (2, 2), (4, 2), (6, 1))
+SPANS = ((0, 1), (1, 2), (3, 2), (5, 2))
 CHUNKS = len(SPANS)
 WALK = 32
 OCC = 100
@@ -343,8 +343,8 @@
             if right > 0 and left < 128:
                 tile = jnp.where((lanes >= left) & (lanes < right), shifted[w], tile)
         xg1[t, chol] = tile.astype(bf16)
-    for j in range(CHUNKS):
-        ag_start(0, xg1, j)
+    ag_start(0, xg1, 0)
+    ag_start(0, xg1, 1)
 
     @pl.loop(1, 16)
     def _(d):
@@ -360,6 +360,7 @@
         f_copy(d, True).start()
 
     ag_relay(0, xg1, 0)
+    ag_start(0, xg1, 2)
 
     @pl.loop(1, WALK)
     def _(d):
@@ -380,6 +381,7 @@
             )
 
     ag_relay(0, xg1, 1)
+    ag_start(0, xg1, 3)
     own_l.wait()
     l_got.wait_recv()
 

time: 93.3 us -> 90.2 us (0.967)
  Pallas kernels: 89.7 us -> 86.5 us
    pallas_call x1, Pallas kernels: 89.7 us -> 86.5 us  [per_device(): pl.pallas_call(body, out_shape=jax.ShapeDtypeStruct((8, 64, OCC), bf16),...]
where the time goes in v5:
time: 90.2 us; the launch traced here: 90 us
  Pallas kernels  86.5 us (96%)
  local copies, waits for them, and re-layouts  3.46 us (4%)
    pallas_call x1, Pallas kernels, per_device(): pl.pallas_call(body, out_shape=jax.ShapeDtypeStruct((8, 64, OCC), bf16),...  86.5 us
    unnamed x2, local copies, waits for them, and re-layouts  2.65 us

profile of v5, /device:TPU:1, one launch (start us, length us, event | category | flops | bytes accessed | tf_op | source)
XLA Modules:
  0.0 90.0 jit_solution(11762339985369220597)
XLA Ops:
  0.0 1.1 %copy.9 = bf16[2,100,1024]{2,1,0:T(8,128)(2,1)S(1)} copy(bf16[2,100,1024]{2,0,1:T(2,128)(2,1)} %param.9) | data formatting | bytes 819200 | tf_op args[1]
  1.1 0.8 pad.4.half_ref
  1.9 86.5 %shard_map.82 = bf16[8,64,100]{2,1,0:T(8,128)(2,1)} custom-call(bf16[2,8,2,64,1024]{4,3,2,1,0:T(8,128)(2,1)} %bitcast.6, bf16[2,112,1024]{2,1,0:T(8,128)(2,1)} %pad.4.half_ref, bf16[8,64,100]{2,1,0:T(8,128)(2,1)} %bitcast.7, bf16[8,64,100]{2,1,0:T(8,128)(2,1)} %bitcast.8, f32[2,8]{1,0:T(2,128)} %bitcast.9, f32[4000]{0:T(1024)} %mean_ref.1, s32[2]{0:T(128)} %index_ref.1, ...), custom_call_target="tpu_custom_call" | custom-call | flops 8600000512 | bytes 6000000 | tf_op jit(solution)/shard_map/pallas_call | solution.py:474
  88.4 1.6 %copy.11 = bf16[8,100,64]{1,2,0:T(8,128)(2,1)} copy(bf16[8,100,64]{1,2,0:T(8,128)(2,1)} %bitcast.5) | data formatting | bytes 204800

commit v6 on v5

--- a/solution.py
+++ b/solution.py
@@ -429,10 +429,7 @@
     mm2(2)
     finish(1)
     mm2(3)
-    finish(2)
-    finish(3)
-
-    for w in range(8):
+    def unpack(w):
         t, start = (OCC * w) // 128, (OCC * w) % 128
         if start:
             mixed = jnp.where(lanes >= start, first[t], first[min(t + 1, TILES - 1)])
@@ -441,6 +438,7 @@
             mixed = first[t]
         out_ref[w] = mixed[:, 0:OCC].astype(bf16)
 
+    late = ((1, CHUNKS - 2), (1, CHUNKS - 1))
     g_copy.wait_send()
     l_copy.wait_send()
     for k in range(7):
@@ -454,7 +452,8 @@
         for j in range(CHUNKS):
             for k in range(7):
                 ag_send(ph, xg, j, k).wait_send()
-                rs_copy(ph, j, k).wait_send()
+                if (ph, j) not in late:
+                    rs_copy(ph, j, k).wait_send()
             for k in range(8):
                 sib(ph, xg, j, k, core).wait_send()
 
@@ -464,6 +463,16 @@
         z_copy(d, True).wait_send()
         y_copy(d, True).wait_send()
         f_copy(d, True).wait_send()
+
+    finish(2)
+    for w in range(6):
+        unpack(w)
+    finish(3)
+    for w in range(6, 8):
+        unpack(w)
+    for ph, j in late:
+        for k in range(7):
+            rs_copy(ph, j, k).wait_send()
 
 
 def per_device(

time: 90.2 us -> 89.5 us (level)
  no operation moved by 1% of the time
where the time goes in v6:
time: 89.5 us; the launch traced here: 89.3 us
  Pallas kernels  85.8 us (96%)
  local copies, waits for them, and re-layouts  3.46 us (4%)
    pallas_call x1, Pallas kernels, per_device(): pl.pallas_call(body, out_shape=jax.ShapeDtypeStruct((8, 64, OCC), bf16),...  85.8 us
    unnamed x2, local copies, waits for them, and re-layouts  2.65 us

profile of v6, /device:TPU:1, one launch (start us, length us, event | category | flops | bytes accessed | tf_op | source)
XLA Modules:
  0.0 89.3 jit_solution(12663002755321121741)
XLA Ops:
  0.0 1.1 %copy.9 = bf16[2,100,1024]{2,1,0:T(8,128)(2,1)S(1)} copy(bf16[2,100,1024]{2,0,1:T(2,128)(2,1)} %param.9) | data formatting | bytes 819200 | tf_op args[1]
  1.1 0.8 pad.4.half_ref
  1.9 85.8 %shard_map.82 = bf16[8,64,100]{2,1,0:T(8,128)(2,1)} custom-call(bf16[2,8,2,64,1024]{4,3,2,1,0:T(8,128)(2,1)} %bitcast.6, bf16[2,112,1024]{2,1,0:T(8,128)(2,1)} %pad.4.half_ref, bf16[8,64,100]{2,1,0:T(8,128)(2,1)} %bitcast.7, bf16[8,64,100]{2,1,0:T(8,128)(2,1)} %bitcast.8, f32[2,8]{1,0:T(2,128)} %bitcast.9, f32[4000]{0:T(1024)} %mean_ref.1, s32[2]{0:T(128)} %index_ref.1, ...), custom_call_target="tpu_custom_call" | custom-call | flops 8600000512 | bytes 6000000 | tf_op jit(solution)/shard_map/pallas_call | solution.py:483
  87.7 1.6 %copy.11 = bf16[8,100,64]{1,2,0:T(8,128)(2,1)} copy(bf16[8,100,64]{1,2,0:T(8,128)(2,1)} %bitcast.5) | data formatting | bytes 204800
